TPU v7x, 32 devices: a whole 2x2x4 slice. The times are simulated.
32 devices in a mesh: slices: 2 (over y), scan: 4 (over z), band: 2 (over x), pix: 2 (over core).
Axes of the slice: x: 2, y: 2, z: 4, core: 2. Of those that a mesh axis runs over, the one named last changes fastest.
Arguments:
- frames: bfloat16 [1024, 524288], P(('slices', 'scan'), ('band', 'pix')), parts along dimension 0, may hold values from -6 to 6
- pixel_weight: bfloat16 [524288], P(('band', 'pix')), may hold values from 0.29882812 to 3
- pixel_slot: int32 [524288], P(('band', 'pix')), may hold values from 0 to 127
- block_tile: int32 [4096], P(('band', 'pix')), may hold values from 0 to 15
- spectra: float32 [64, 2048], P(None, ('scan', 'band', 'pix')), may hold values from 0.1 to 1
- ray_index: int32 [4, 512, 512], P(None, ('scan', 'pix')), may hold values from 0 to 127, as said below
Outputs:
- images: float32 [128, 512, 512], P(('slices', 'band'), ('scan', 'pix')), parts along dimension 0
There are 2 independent parts, one for each index of `slices`. A program takes and returns all parts, laid end to end along the dimension named above; an argument that names none is the same for every part. Nothing has to cross between parts.
Inputs may be any that keep to these rules, and one draw needn't show every extreme that they name: `ray_index`: every translation index is met by at least one image pixel at every angle.
All inputs are finite; a program needn't handle non-finite values.
Results may differ from a plain program's by a relative error of at most 0.0003.
Values sent between devices are 32-bit elements; how exact they have to be, the bound alone decides.
A program may use at most 320 MiB of HBM per device.

v0:
```python
import jax
import jax.numpy as jnp
from jax import lax
from jax.sharding import PartitionSpec as P

TILE = 128
Q = 2048
ITERS = 3


RELAX = 1.5


def shards(frames, pixel_weight, pixel_slot, block_tile, spectra, ray_index):
    highest = lax.Precision.HIGHEST
    scan_count = lax.axis_size("scan")
    band_count = lax.axis_size("band")
    pair_count = band_count * lax.axis_size("pix")
    pos_local, pix_local = frames.shape
    block_count = pix_local // TILE
    comp_total, bin_local = spectra.shape
    angles, row_local, img_width = ray_index.shape
    slot_table = pixel_slot.reshape(block_count, TILE)
    weight_table = pixel_weight.reshape(block_count, TILE)
    spread = jnp.where(
        slot_table[:, :, None] == jnp.arange(TILE, dtype=jnp.int32)[None, None, :],
        weight_table[:, :, None],
        jnp.zeros((), jnp.bfloat16),
    )
    blocked = jnp.einsum(
        "pbk,bkl->bpl",
        frames.reshape(pos_local, block_count, TILE),
        spread,
        preferred_element_type=jnp.float32,
    )
    tile_total = Q // TILE
    tile_onehot = (block_tile[:, None] == jnp.arange(tile_total, dtype=jnp.int32)[None, :]).astype(
        jnp.float32
    )
    binned = jnp.einsum("bpl,bt->ptl", blocked, tile_onehot, precision=highest)
    partial_bins = binned.reshape(pos_local, scan_count, pair_count, bin_local)
    pos_total = pos_local * scan_count
    translations = pos_total // angles
    pixels_local = row_local * img_width
    ray_flat = ray_index.reshape(angles, pixels_local)
    ray_hits = (
        ray_flat[:, None, :] == jnp.arange(translations, dtype=jnp.int32)[None, :, None]
    ).astype(jnp.float32)
    count_part = jnp.sum(ray_hits, axis=2).reshape(pos_total) / band_count
    comp_local = comp_total // band_count
    first_comp = lax.axis_index("band") * comp_local
    regrouped = lax.all_to_all(partial_bins, "scan", split_axis=1, concat_axis=0, tiled=True)
    integrated = lax.psum_scatter(regrouped, ("band", "pix"), scatter_dimension=2, tiled=True)
    integrated = integrated.reshape(pos_total, bin_local)
    moments_part = jnp.dot(integrated, spectra.T, precision=highest)
    gram_part = jnp.dot(spectra, spectra.T, precision=highest)
    moments, gram_total, ray_count = lax.psum(
        (moments_part, gram_part, count_part), ("scan", "band", "pix")
    )
    factor = jnp.linalg.cholesky(gram_total)
    all_coefficients = jax.scipy.linalg.cho_solve((factor, True), moments.T).T
    coefficients = lax.dynamic_slice_in_dim(all_coefficients, first_comp, comp_local, 1)
    images = jnp.zeros((comp_local, pixels_local), jnp.float32)
    for sweep in range(ITERS):
        if sweep == 0:
            residual = coefficients
        else:
            projected_part = (
                jnp.einsum("atn,cn->atc", ray_hits, images, precision=highest).reshape(
                    pos_total, comp_local
                )
                / img_width
            )
            projected = lax.psum(projected_part, ("scan", "pix"))
            residual = coefficients - projected
        weighted_res = (residual / ray_count[:, None]).reshape(angles, translations, comp_local)
        backward = jnp.einsum("atn,atc->cn", ray_hits, weighted_res, precision=highest)
        images = images + RELAX * img_width / angles * backward
    return images.reshape(comp_local, row_local, img_width)


def solution(mesh):
    return jax.shard_map(
        shards,
        mesh=mesh,
        in_specs=(
            P(("slices", "scan"), ("band", "pix")),
            P(("band", "pix")),
            P(("band", "pix")),
            P(("band", "pix")),
            P(None, ("scan", "band", "pix")),
            P(None, ("scan", "pix"), None),
        ),
        out_specs=P(("slices", "band"), ("scan", "pix"), None),
        check_vma=False,
    )
```

profile of v0, /device:TPU:0, one launch (start us, length us, event | category | flops | bytes accessed | tf_op | source)
XLA Modules:
  0.0 597.2 jit_solution(15088554760502070504)
XLA Ops:
  6.5 38.7 %fusion.24 = f32[1024,128,128]{1,2,0:T(8,128)} fusion(s32[1024,128]{1,0:T(8,128)} %bitcast.123, bf16[1024,128]{1,0:T(8,128)(2,1)} %bitcast.124, bf16[128,131072]{1,0:T(8,128)(2,1)} %param.6), kind=kOutput, calls=%fused_computation.26 | convolution fusion | flops 4328521728 | bytes 101449728 | tf_op jit(solution)/shard_map/pbk,bkl->bpl/dot_general | solution.py:30
  45.2 65.9 %copy.25 = f32[1024,128,128]{2,0,1:T(8,128)} copy(f32[1024,128,128]{1,2,0:T(8,128)} %fusion.24) | data formatting | bytes 134217728 | tf_op jit(solution)/shard_map/pbk,bkl->bpl/dot_general | solution.py:30
  111.1 27.8 %fusion.54 = f32[16,128,128]{2,0,1:T(8,128)S(1)} fusion(f32[1024,128,128]{2,0,1:T(8,128)} %copy.25, s32[1024]{0:T(1024)S(1)} %copy-done.2), kind=kOutput, calls=%fused_computation.50 | convolution fusion | flops 3221241856 | bytes 68161536 | tf_op jit(solution)/shard_map/bpl,bt->ptl/dot_general | solution.py:40
  139.3 31.8 %all_to_all.18 = f32[128,4,4,128]{3,0,2,1:T(8,128)S(1)} all-to-all(f32[128,4,4,128]{3,0,2,1:T(8,128)S(1)} %copy.26), channel_id=1, replica_groups=mesh['slices'=2,'scan'=4,'band'=2,'pix'=2] {'scan'}, dimensions={1} | all-to-all | bytes 2097152 | tf_op jit(solution)/shard_map/all_to_all | solution.py:52
  171.1 1.1 copy.27
  172.6 7.9 %convert_reduce_fusion = f32[4,128]{1,0:T(4,128)S(1)} fusion(s32[4,32768]{1,0:T(4,128)S(1)} %bitcast.114), kind=kLoop, calls=%fused_computation | loop fusion | flops 50331136 | bytes 526336 | tf_op jit(solution)/shard_map/reduce_sum | solution.py:49
  180.7 59.0 %all-reduce = (f32[64,64]{0,1:T(8,128)S(1)}, f32[512]{0:T(512)S(1)}) all-reduce(f32[64,64]{0,1:T(8,128)S(1)} %fusion.64, f32[512]{0:T(512)S(1)} %multiply_bitcast_fusion), channel_id=1, replica_groups=mesh['slices'=2,'scan'=4,'band'=2,'pix'=2] {'scan','band','pix'}, use_global_device_ids=true, to_apply=%region_0.1 | all-reduce | flops 4608 | bytes 36864 | tf_op jit(solution)/shard_map/psum | solution.py:57
  239.9 5.9 cholesky.16
  245.8 0.7 compare_reduce_fusion
  246.5 2.0 fusion.45
  248.8 0.6 fusion.56
  249.4 4.9 custom-call.10
  254.3 78.6 %all-reduce.5.cloned.1.call-done = f32[512,64]{0,1:T(8,128)} async-done(((f32[512,64]{0,1:T(8,128)}), f32[512,64]{0,1:T(8,128)}) %all-reduce.5.cloned.1.call-update) | async-done | bytes 131088 | tf_op jit(solution)/shard_map/psum | solution.py:57
  332.9 1.2 fusion.59
  334.4 24.3 %fusion.11 = f32[32,32768]{1,0:T(8,128)S(1)} fusion(s32[4,32768]{1,0:T(4,128)S(1)} %bitcast.115, f32[512,64]{0,1:T(8,128)S(1)} %fusion.57, s32[]{:T(128)S(6)} %select_n.13, f32[512]{0:T(512)S(1)} %get-tuple-element.6), kind=kOutput, calls=%fused_computation.14 | convolution fusion | flops 6460293120 | bytes 4786180 | tf_op jit(solution)/shard_map/atn,atc->cn/dot_general | solution.py:77
  358.7 33.2 %fusion.36 = f32[4,4,8,128]{3,2,1,0:T(8,128)S(1)} fusion(f32[32,32768]{1,0:T(8,128)S(1)} %fusion.11, s32[4,32768]{1,0:T(4,128)S(1)} %bitcast.116), kind=kOutput, calls=%fused_computation.32 | convolution fusion | flops 6459244544 | bytes 4784128 | tf_op jit(solution)/shard_map/atn,cn->atc/dot_general | solution.py:69
  391.8 0.6 copy.63
  392.5 55.3 %all-reduce.7.cloned.1.call-done = f32[512,32]{0,1:T(8,128)} async-done(((f32[512,32]{0,1:T(8,128)}), f32[512,32]{0,1:T(8,128)}) %all-reduce.7.cloned.1.call-update) | async-done | bytes 65552 | tf_op jit(solution)/shard_map/psum | solution.py:74
  447.9 25.7 %fusion.12 = f32[32,32768]{1,0:T(8,128)S(1)} fusion(f32[32,32768]{1,0:T(8,128)} %copy-done.4, s32[4,32768]{1,0:T(4,128)S(1)} %bitcast.117, f32[512,32]{0,1:T(8,128)} %all-reduce.7.cloned.1.call-done, f32[512,64]{0,1:T(8,128)S(1)} %fusion.57, s32[]{:T(128)S(6)} %select_n.13, f32[512]{0:T(512)S(1)} %get-tuple-element.6), kind=kOutput, calls=%fused_computation.15 | convolution fusion | flops 6461358080 | bytes 9046020 | tf_op jit(solution)/shard_map/atn,atc->cn/dot_general | solution.py:77
  473.6 33.0 %fusion.42 = f32[4,4,8,128]{3,2,1,0:T(8,128)S(1)} fusion(f32[32,32768]{1,0:T(8,128)S(1)} %fusion.12, s32[4,32768]{1,0:T(4,128)S(1)} %bitcast.118), kind=kOutput, calls=%fused_computation.34 | convolution fusion | flops 6459244544 | bytes 4784128 | tf_op jit(solution)/shard_map/atn,cn->atc/dot_general | solution.py:69
  506.7 0.6 copy.62
  507.3 52.8 %all-reduce.9.cloned.1.call-done = f32[512,32]{0,1:T(8,128)} async-done(((f32[512,32]{0,1:T(8,128)}), f32[512,32]{0,1:T(8,128)}) %all-reduce.9.cloned.1.call-update) | async-done | bytes 65552 | tf_op jit(solution)/shard_map/psum | solution.py:74
  560.1 25.7 %fusion.13 = f32[32,32768]{1,0:T(8,128)S(1)} fusion(f32[32,32768]{1,0:T(8,128)} %copy-done.3, s32[4,32768]{1,0:T(4,128)S(1)} %bitcast.119, f32[512,32]{0,1:T(8,128)} %all-reduce.9.cloned.1.call-done, f32[512,64]{0,1:T(8,128)S(1)} %fusion.57, s32[]{:T(128)S(6)} %select_n.13, f32[512]{0:T(512)S(1)} %get-tuple-element.6), kind=kOutput, calls=%fused_computation.16 | convolution fusion | flops 6461358080 | bytes 9046020 | tf_op jit(solution)/shard_map/atn,atc->cn/dot_general | solution.py:77
  585.8 4.4 copy.41
  (27 shorter events, 1.7 us)
Async XLA Ops:
  6.5 174.0 %copy-start = (f32[64,128]{1,0:T(8,128)S(1)}, f32[64,128]{1,0:T(8,128)}, u32[]{:S(2)}) copy-start(f32[64,128]{1,0:T(8,128)} %param.10) | copy-start | bytes 98308
  6.5 239.9 %reduce-scatter.2.cloned.1.call-start = ((), (), s32[]{:S(2)}) async-start(), calls=%async_computation.2 | async-start | bytes 1310720 | tf_op jit(solution)/shard_map/reduce_scatter | solution.py:53
  45.2 65.9 %copy-start.2 = (s32[1024]{0:T(1024)S(1)}, s32[1024]{0:T(1024)}, u32[]{:S(2)}) copy-start(s32[1024]{0:T(1024)} %param.9) | copy-start | bytes 12292
  111.1 61.2 %copy-start.1 = (s32[4,64,512]{2,1,0:T(8,128)S(1)}, s32[4,64,512]{2,1,0:T(8,128)}, u32[]{:S(2)}) copy-start(s32[4,64,512]{2,1,0:T(8,128)} %param.11) | copy-start | bytes 1572868
  172.2 160.7 %all-reduce.5.cloned.1.call-start = ((), (), s32[]{:S(2)}) async-start(), calls=%async_computation.3 | async-start | bytes 262144 | tf_op jit(solution)/shard_map/psum | solution.py:57
  248.5 199.4 %all-reduce.7.cloned.1.call-start = ((), (), s32[]{:S(2)}) async-start(), calls=%async_computation.4 | async-start | bytes 131072 | tf_op jit(solution)/shard_map/psum | solution.py:74
  358.7 33.8 %copy-start.4 = (f32[32,32768]{1,0:T(8,128)}, f32[32,32768]{1,0:T(8,128)S(1)}, u32[]{:S(2)}) copy-start(f32[32,32768]{1,0:T(8,128)S(1)} %fusion.11) | copy-start | bytes 12582916
  392.5 167.6 %all-reduce.9.cloned.1.call-start = ((), (), s32[]{:S(2)}) async-start(), calls=%async_computation.5 | async-start | bytes 131072 | tf_op jit(solution)/shard_map/psum | solution.py:74
  473.6 33.7 %copy-start.3 = (f32[32,32768]{1,0:T(8,128)}, f32[32,32768]{1,0:T(8,128)S(1)}, u32[]{:S(2)}) copy-start(f32[32,32768]{1,0:T(8,128)S(1)} %fusion.12) | copy-start | bytes 12582916
Sparse Core Ops, SparseCore 0:
  172.3 24.1 reduce-scatter.1
  248.6 84.1 all-reduce.4
  392.6 55.2 all-reduce.6
  507.4 52.6 all-reduce.8
where the time goes:
time: 606 us; the launch traced here: 597 us
  matrix products  212 us (35%)
  waiting for transfers between devices  187 us (31%)
  blocking collectives  90.9 us (15%)
  local copies, waits for them, and re-layouts  73.4 us (12%)
  other arithmetic  20 us (3%)
  between operations  13.7 us (2%)
    psum x2, waiting for transfers between devices, shards(): projected = lax.psum(projected_part, ('scan', 'pix'))  108 us
    psum x1, waiting for transfers between devices, shards(): lax.psum((moments_part, gram_part, count_part), ('scan', 'band', 'pix'))  78.6 us
    dot_general x3, matrix products, shards(): jnp.einsum('atn,atc->cn', ray_hits, weighted_res, precision=highest)  75.7 us
    dot_general x2, matrix products, shards(): jnp.einsum('atn,cn->atc', ray_hits, images, precision=highest)  66.2 us
    dot_general x1, local copies, waits for them, and re-layouts, shards(): jnp.einsum('pbk,bkl->bpl', frames.reshape(pos_local, block_count, TILE),...  65.9 us
    psum x1, blocking collectives, shards(): lax.psum((moments_part, gram_part, count_part), ('scan', 'band', 'pix'))  59 us
    dot_general x1, matrix products, shards(): jnp.einsum('pbk,bkl->bpl', frames.reshape(pos_local, block_count, TILE),...  38.7 us
    all_to_all x1, blocking collectives, shards(): lax.all_to_all(partial_bins, 'scan', split_axis=1, concat_axis=0, tiled=T...  31.8 us
  transfers between devices with their start and end apart: 4, of which 3 were waited for; matrix products, arithmetic and copies ran while one was open for 3% of the time, Pallas kernels for 0%

commit v1 on v0

v1 whole, which is shorter than its diff:
```python
import functools

import jax
import jax.numpy as jnp
from jax import lax
from jax.experimental import pallas as pl
from jax.experimental.pallas import tpu as pltpu
from jax.sharding import PartitionSpec as P

TILE = 128
Q = 2048
ITERS = 3
RELAX = 1.5
CHUNK = 8192
NT_DIMS = (((1,), (1,)), ((), ()))


def bin_kernel(tile_ref, frames_ref, slot_ref, weight_ref, out_ref, *, blocks):
    step = pl.program_id(0)
    pos = frames_ref.shape[0]

    @pl.when(step == 0)
    def _():
        out_ref[...] = jnp.zeros_like(out_ref)

    row_id = lax.broadcasted_iota(jnp.int32, (TILE, TILE), 0).astype(jnp.bfloat16)
    zero = jnp.zeros((TILE, TILE), jnp.bfloat16)
    for pair in range(blocks // 2):
        parts = []
        for half in range(2):
            b = 2 * pair + half
            slot = jnp.broadcast_to(slot_ref[b : b + 1, :].astype(jnp.float32), (TILE, TILE))
            weight = jnp.broadcast_to(weight_ref[b : b + 1, :].astype(jnp.float32), (TILE, TILE))
            spread = jnp.where(slot.astype(jnp.bfloat16) == row_id, weight.astype(jnp.bfloat16), zero)
            parts.append(
                jnp.concatenate([spread, zero] if half == 0 else [zero, spread], axis=1)
            )
        spread = jnp.concatenate(parts, axis=0)
        both = lax.dot_general(
            frames_ref[:, 2 * pair * TILE : (2 * pair + 2) * TILE],
            spread,
            NT_DIMS,
            preferred_element_type=jnp.float32,
        )
        for half in range(2):
            t = tile_ref[step * blocks + 2 * pair + half]
            out_ref[t] += both[:, half * TILE : (half + 1) * TILE]


def bin_frames(frames, pixel_weight, pixel_slot, block_tile):
    pos, pixels = frames.shape
    chunk = min(CHUNK, pixels)
    blocks = chunk // TILE
    tiles = Q // TILE
    return pl.pallas_call(
        functools.partial(bin_kernel, blocks=blocks),
        grid_spec=pltpu.PrefetchScalarGridSpec(
            num_scalar_prefetch=1,
            grid=(pixels // chunk,),
            in_specs=[
                pl.BlockSpec((pos, chunk), lambda i, t: (0, i)),
                pl.BlockSpec((blocks, TILE), lambda i, t: (i, 0)),
                pl.BlockSpec((blocks, TILE), lambda i, t: (i, 0)),
            ],
            out_specs=pl.BlockSpec((tiles, pos, TILE), lambda i, t: (0, 0, 0)),
        ),
        out_shape=jax.ShapeDtypeStruct((tiles, pos, TILE), jnp.float32),
        compiler_params=pltpu.CompilerParams(vmem_limit_bytes=40 * 1024 * 1024),
        cost_estimate=pl.CostEstimate(
            flops=4 * pos * pixels * TILE, bytes_accessed=2 * pos * pixels, transcendentals=0
        ),
        name="bin_frames",
    )(
        block_tile,
        frames,
        pixel_slot.reshape(-1, TILE),
        pixel_weight.reshape(-1, TILE),
    )


def pair_kernel(ray_ref, out_ref, *, translations):
    angles, rows, width = ray_ref.shape
    row_id = lax.broadcasted_iota(jnp.int32, (translations, width), 0).astype(jnp.bfloat16)
    one = jnp.ones((translations, width), jnp.bfloat16)
    zero = jnp.zeros((translations, width), jnp.bfloat16)
    out_ref[...] = jnp.zeros_like(out_ref)
    for r in range(rows):
        hits = []
        for a in range(angles):
            index = jnp.broadcast_to(
                ray_ref[a, r : r + 1, :].astype(jnp.float32), (translations, width)
            ).astype(jnp.bfloat16)
            hits.append(jnp.where(index == row_id, one, zero))
        hits = jnp.concatenate(hits, axis=0)
        out_ref[...] += lax.dot_general(hits, hits, NT_DIMS, preferred_element_type=jnp.float32)


def pair_counts(rays, translations):
    angles, rows, width = rays.shape
    total = angles * translations
    return pl.pallas_call(
        functools.partial(pair_kernel, translations=translations),
        out_shape=jax.ShapeDtypeStruct((total, total), jnp.float32),
        compiler_params=pltpu.CompilerParams(vmem_limit_bytes=40 * 1024 * 1024),
        cost_estimate=pl.CostEstimate(
            flops=2 * total * total * rows * width, bytes_accessed=4 * total * total, transcendentals=0
        ),
        name="pair_counts",
    )(rays)


def back_kernel(table_ref, ray_ref, out_ref, *, translations):
    comps, rows, width = out_ref.shape
    angles = ray_ref.shape[0]

    def one_comp(c, carry):
        rows_of = table_ref[c]
        tables = [jnp.broadcast_to(rows_of[a : a + 1, :], (8, translations)) for a in range(angles)]
        for r in range(0, rows, 8):
            for w in range(0, width, translations):
                value = None
                for a in range(angles):
                    index = ray_ref[a, r : r + 8, w : w + translations]
                    got = jnp.take_along_axis(
                        tables[a], index, axis=1, mode="promise_in_bounds"
                    )
                    value = got if value is None else value + got
                out_ref[c, r : r + 8, w : w + translations] = value
        return carry

    lax.fori_loop(0, comps, one_comp, 0)


def back_project(table, rays, translations):
    comps = table.shape[0]
    angles, rows, width = rays.shape
    group = min(8, comps)
    return pl.pallas_call(
        functools.partial(back_kernel, translations=translations),
        grid=(comps // group,),
        in_specs=[
            pl.BlockSpec((group, angles, translations), lambda i: (i, 0, 0)),
            pl.BlockSpec((angles, rows, width), lambda i: (0, 0, 0)),
        ],
        out_specs=pl.BlockSpec((group, rows, width), lambda i: (i, 0, 0)),
        out_shape=jax.ShapeDtypeStruct((comps, rows, width), jnp.float32),
        compiler_params=pltpu.CompilerParams(vmem_limit_bytes=40 * 1024 * 1024),
        cost_estimate=pl.CostEstimate(
            flops=comps * angles * rows * width, bytes_accessed=4 * comps * rows * width, transcendentals=0
        ),
        name="back_project",
    )(table.reshape(comps, angles, translations), rays)


def shards(frames, pixel_weight, pixel_slot, block_tile, spectra, ray_index):
    highest = lax.Precision.HIGHEST
    scan_count = lax.axis_size("scan")
    band_count = lax.axis_size("band")
    pos_local, pix_local = frames.shape
    comp_total, bin_local = spectra.shape
    angles, row_local, img_width = ray_index.shape
    pos_total = pos_local * scan_count
    translations = pos_total // angles
    comp_local = comp_total // band_count
    first_comp = lax.axis_index("band") * comp_local

    copies = lax.axis_size("slices") * band_count
    copy_id = lax.axis_index("slices") * band_count + lax.axis_index("band")
    share = row_local // copies
    own_rays = lax.dynamic_slice_in_dim(ray_index, copy_id * share, share, 1)
    counts = lax.psum(pair_counts(own_rays, translations), ("slices", "scan", "band", "pix"))
    all_spectra = lax.all_gather(spectra, ("scan", "band", "pix"), axis=1, tiled=True)

    bins = bin_frames(frames, pixel_weight, pixel_slot, block_tile)

    gram = lax.dot_general(all_spectra, all_spectra, NT_DIMS, precision=highest)
    factor = jnp.linalg.cholesky(gram)
    moments_part = jnp.einsum(
        "ctl,tpl->cp", all_spectra.reshape(comp_total, Q // TILE, TILE), bins, precision=highest
    )
    place = lax.axis_index("scan") * pos_local
    moments_wide = lax.dynamic_update_slice_in_dim(
        jnp.zeros((comp_total, pos_total), jnp.float32), moments_part, place, 1
    )
    moments = lax.psum(moments_wide, ("scan", "band", "pix"))
    all_coefficients = jax.scipy.linalg.cho_solve((factor, True), moments)
    coefficients = lax.dynamic_slice_in_dim(all_coefficients, first_comp, comp_local, 0)
    ray_count = jnp.diagonal(counts)[None, :]
    total = jnp.zeros((comp_local, pos_total), jnp.float32)
    for sweep in range(ITERS):
        residual = coefficients
        if sweep > 0:
            residual = coefficients - (RELAX / angles) * jnp.dot(total, counts, precision=highest)
        total = total + residual / ray_count
    return back_project((RELAX * img_width / angles) * total, ray_index, translations)


def solution(mesh):
    return jax.shard_map(
        shards,
        mesh=mesh,
        in_specs=(
            P(("slices", "scan"), ("band", "pix")),
            P(("band", "pix")),
            P(("band", "pix")),
            P(("band", "pix")),
            P(None, ("scan", "band", "pix")),
            P(None, ("scan", "pix"), None),
        ),
        out_specs=P(("slices", "band"), ("scan", "pix"), None),
        check_vma=False,
    )
```

time: 606 us -> 320 us (0.53); the launches traced: 597 us -> 319 us
  matrix products: 212 us -> 7.14 us
  blocking collectives: 90.9 us -> 24.9 us
  local copies, waits for them, and re-layouts: 73.4 us -> 11.9 us
  Pallas kernels: 0 us -> 47.5 us
  waiting for transfers between devices: 187 us -> 202 us
  other arithmetic: 20 us -> 12.1 us
    dot_general x9 -> x4, matrix products: 211 us -> 5.66 us  [the longest x2 3.88 us: shards(): jnp.dot(total, counts, precision=highest)]
    dot_general x1, local copies, waits for them, and re-layouts: 65.9 us -> 0.07 us  [shards(): gram = lax.dot_general(all_spectra, all_spectra, NT_DIMS, precision=highest)]
    psum x1 -> x0, blocking collectives: 59 us -> none  [shards(): lax.psum((moments_part, gram_part, count_part), ('scan', 'band', 'pix'))]
    pallas_call x0 -> x3, Pallas kernels: none -> 47.5 us  [the longest x1 27.4 us: bin_frames(): pl.pallas_call(functools.partial(bin_kernel, blocks=blocks), grid_spec=pl...]
    all_to_all x1 -> x0, blocking collectives: 31.8 us -> none  [shards(): lax.all_to_all(partial_bins, 'scan', split_axis=1, concat_axis=0, tiled=T...]
    all_gather x0 -> x1, blocking collectives: none -> 24.9 us  [shards(): lax.all_gather(spectra, ('scan', 'band', 'pix'), axis=1, tiled=True)]
    psum x3 -> x2, waiting for transfers between devices: 187 us -> 202 us  [the longest x1 135 us: shards(): lax.psum(pair_counts(own_rays, translations), ('slices', 'scan', 'band',...]
    gather x0 -> x1, local copies, waits for them, and re-layouts: none -> 8.42 us  [shards(): ray_count = jnp.diagonal(counts)[None, :]]
  transfers between devices with their start and end apart: 4 -> 2, of which waited for: 3 -> 2; matrix products, arithmetic and copies ran while one was open for 3% -> 4% of each run, Pallas kernels for 0% -> 2%
where the time goes in v1:
time: 320 us; the launch traced here: 319 us
  waiting for transfers between devices  202 us (63%)
  Pallas kernels  47.5 us (15%)
  blocking collectives  24.9 us (8%)
  between operations  13.5 us (4%)
  other arithmetic  12.1 us (4%)
  local copies, waits for them, and re-layouts  11.9 us (4%)
  matrix products  7.14 us (2%)
    psum x1, waiting for transfers between devices, shards(): lax.psum(pair_counts(own_rays, translations), ('slices', 'scan', 'band',...  135 us
    psum x1, waiting for transfers between devices, shards(): moments = lax.psum(moments_wide, ('scan', 'band', 'pix'))  66.2 us
    pallas_call x1, Pallas kernels, bin_frames(): pl.pallas_call(functools.partial(bin_kernel, blocks=blocks), grid_spec=pl...  27.4 us
    all_gather x1, blocking collectives, shards(): lax.all_gather(spectra, ('scan', 'band', 'pix'), axis=1, tiled=True)  24.9 us
    pallas_call x1, Pallas kernels, back_project(): pl.pallas_call(functools.partial(back_kernel, translations=translations),...  14.7 us
    gather x1, local copies, waits for them, and re-layouts, shards(): ray_count = jnp.diagonal(counts)[None, :]  8.42 us
    another operation x3, other arithmetic, shards(): factor = jnp.linalg.cholesky(gram)  6.55 us
  transfers between devices with their start and end apart: 2, of which 2 were waited for; matrix products, arithmetic and copies ran while one was open for 4% of the time, Pallas kernels for 2%

profile of v1, /device:TPU:0, one launch (start us, length us, event | category | flops | bytes accessed | tf_op | source)
XLA Modules:
  0.0 318.7 jit_solution(4027790413995605859)
XLA Ops:
  6.5 24.9 %all_gather.3 = f32[64,2048]{1,0:T(8,128)S(1)} all-gather(f32[64,128]{1,0:T(8,128)} %param.10), channel_id=1, replica_groups=mesh['slices'=2,'scan'=4,'band'=2,'pix'=2] {'scan','band','pix'}, dimensions={1}, use_global_device_ids=true | all-gather | bytes 557056 | tf_op jit(solution)/shard_map/all_gather | solution.py:172
  31.4 1.0 copy-done.1
  32.5 0.9 copy-done.2
  33.4 0.7 copy-done.3
  34.1 27.4 %bin_frames.1 = f32[16,128,128]{2,1,0:T(8,128)S(1)} custom-call(s32[1024]{0:T(1024)S(1)} %copy-done.3, bf16[128,131072]{1,0:T(8,128)(2,1)} %frames_ref.1, s32[1024,128]{1,0:T(8,128)S(1)} %bitcast.35, bf16[1024,128]{1,0:T(8,128)(2,1)S(1)} %bitcast.36), custom_call_target="tpu_custom_call" | custom-call | flops 8589934592 | bytes 33554432 | tf_op jit(solution)/shard_map/bin_frames/pallas_call | solution.py:55
  61.5 1.2 fusion.7
  62.8 0.7 copy-done.4
  63.4 0.0 all-reduce.3.cloned.1.call-update
  63.4 0.0 all-reduce.5.cloned.1.call-start
  63.5 5.5 %pair_counts.1 = f32[512,512]{1,0:T(8,128)} custom-call(s32[4,16,512]{2,1,0:T(8,128)S(1)} %constant_dynamic-slice_fusion.ray_ref), custom_call_target="tpu_custom_call" | custom-call | flops 4294967296 | bytes 1048576 | tf_op jit(solution)/shard_map/pair_counts/pallas_call | solution.py:101
  69.0 0.6 fusion.20
  69.6 0.1 copy.8
  69.7 5.8 %cholesky.16 = f32[64,64]{1,0:T(8,128)S(1)} custom-call(f32[64,64]{1,0:T(8,128)S(1)} %fusion.17), custom_call_target="Cholesky" | custom-call | tf_op jit(solution)/shard_map/jit(cholesky)/cholesky | solution.py:177
  75.6 0.7 compare_reduce_fusion
  76.3 0.6 fusion.12
  76.9 4.9 %custom-call.10 = f32[1,64,64]{1,2,0:T(8,128)S(1)} custom-call(f32[1,64,64]{2,1,0:T(8,128)S(1)} %fusion.12), custom_call_target="InvertDiagBlocksLowerTriangular" | custom-call | tf_op jit(solution)/shard_map/jit(_cho_solve)/triangular_solve | solution.py:186
  81.8 66.2 %all-reduce.3.cloned.1.call-done = f32[64,512]{1,0:T(8,128)} async-done(((f32[64,512]{1,0:T(8,128)}), f32[64,512]{1,0:T(8,128)}) %all-reduce.3.cloned.1.call-update) | async-done | bytes 131088 | tf_op jit(solution)/shard_map/psum | solution.py:185
  148.0 1.2 fusion.15
  149.3 0.3 fusion.13
  149.5 135.3 %all-reduce.5.cloned.1.call-done = f32[512,512]{1,0:T(8,128)} async-done(((f32[512,512]{1,0:T(8,128)}), f32[512,512]{1,0:T(8,128)}) %all-reduce.5.cloned.1.call-update) | async-done | bytes 1048592 | tf_op jit(solution)/shard_map/psum | solution.py:171
  284.8 8.4 %gather_fusion = f32[512]{0:T(512)S(1)} fusion(f32[512,512]{1,0:T(8,128)} %all-reduce.5.cloned.1.call-done, s32[512]{0:T(512)S(1)} %bitcast.37), kind=kCustom, calls=%fused_computation | custom fusion | bytes 8192 | tf_op jit(solution)/shard_map/jit(diagonal)/cond/branch_0_fun/gather | solution.py:188
  293.3 1.9 fusion.5
  295.2 1.9 fusion.6
  297.2 14.7 %back_project.1 = f32[32,64,512]{2,1,0:T(8,128)} custom-call(f32[32,4,128]{2,1,0:T(4,128)S(1)} %reshape.29.table_ref, s32[4,64,512]{2,1,0:T(8,128)S(1)} %copy-done), custom_call_target="tpu_custom_call" | custom-call | flops 4194304 | bytes 4194304 | tf_op jit(solution)/shard_map/back_project/pallas_call | solution.py:138
  (14 shorter events, 0.1 us)
Async XLA Ops:
  6.5 57.0 %copy-start = (s32[4,64,512]{2,1,0:T(8,128)S(1)}, s32[4,64,512]{2,1,0:T(8,128)}, u32[]{:S(2)}) copy-start(s32[4,64,512]{2,1,0:T(8,128)} %ray_ref.1) | copy-start | bytes 1572868
  6.5 141.5 %all-reduce.3.cloned.1.call-start = ((), (), s32[]{:S(2)}) async-start(), calls=%async_computation | async-start | bytes 262144 | tf_op jit(solution)/shard_map/psum | solution.py:185
  31.4 1.0 copy-start.1
  32.5 0.9 copy-start.2
  33.4 0.7 copy-start.3
  62.7 0.7 copy-start.4
  63.4 221.4 %all-reduce.5.cloned.1.call-start = ((), (), s32[]{:S(2)}) async-start(), calls=%async_computation.1 | async-start | bytes 2097152 | tf_op jit(solution)/shard_map/psum | solution.py:171
Sparse Core Ops, SparseCore 0:
  63.5 84.4 all-reduce.2
  153.2 131.5 all-reduce.4

commit v2 on v1

--- a/solution.py
+++ b/solution.py
@@ -12,6 +12,7 @@
 ITERS = 3
 RELAX = 1.5
 CHUNK = 8192
+MESH = pl.DeviceIdType.MESH
 NT_DIMS = (((1,), (1,)), ((), ()))
 
 
@@ -78,35 +79,239 @@
     )
 
 
-def pair_kernel(ray_ref, out_ref, *, translations):
+def pair_kernel(ray_ref, out_ref, count_ref):
+    step = pl.program_id(0)
     angles, rows, width = ray_ref.shape
-    row_id = lax.broadcasted_iota(jnp.int32, (translations, width), 0).astype(jnp.bfloat16)
-    one = jnp.ones((translations, width), jnp.bfloat16)
-    zero = jnp.zeros((translations, width), jnp.bfloat16)
-    out_ref[...] = jnp.zeros_like(out_ref)
+    nt = out_ref.shape[0] // angles
+    row_id = lax.broadcasted_iota(jnp.int32, (nt, width), 0).astype(jnp.bfloat16)
+    one = jnp.ones((nt, width), jnp.bfloat16)
+    zero = jnp.zeros((nt, width), jnp.bfloat16)
+
+    @pl.when(step == 0)
+    def _():
+        out_ref[...] = jnp.zeros_like(out_ref)
+
+    def meet(left, right):
+        return lax.dot_general(left, right, NT_DIMS, preferred_element_type=jnp.float32)
+
     for r in range(rows):
         hits = []
         for a in range(angles):
-            index = jnp.broadcast_to(
-                ray_ref[a, r : r + 1, :].astype(jnp.float32), (translations, width)
-            ).astype(jnp.bfloat16)
-            hits.append(jnp.where(index == row_id, one, zero))
-        hits = jnp.concatenate(hits, axis=0)
-        out_ref[...] += lax.dot_general(hits, hits, NT_DIMS, preferred_element_type=jnp.float32)
+            index = jnp.broadcast_to(ray_ref[a, r : r + 1, :].astype(jnp.float32), (nt, width))
+            hits.append(jnp.where(index.astype(jnp.bfloat16) == row_id, one, zero))
+        first = jnp.concatenate(hits[:2], axis=0)
+        last = jnp.concatenate(hits[2:], axis=0)
+        out_ref[: 2 * nt, 2 * nt :] += meet(first, last)
+        out_ref[:nt, : 2 * nt] += meet(hits[0], first)
+        out_ref[2 * nt : 3 * nt, 2 * nt :] += meet(hits[2], last)
+
+    @pl.when(step == pl.num_programs(0) - 1)
+    def _():
+        same = lax.broadcasted_iota(jnp.int32, (nt, nt), 0) == lax.broadcasted_iota(jnp.int32, (nt, nt), 1)
+        for base in (0, 2 * nt):
+            block = out_ref[base : base + nt, base : base + 2 * nt]
+            held = jnp.sum(block, axis=0, keepdims=True)
+            count_ref[:, base : base + 2 * nt] = jnp.broadcast_to(held, (8, 2 * nt))
+            out_ref[base + nt : base + 2 * nt, base : base + nt] = block[:, nt:].T
+            out_ref[base + nt : base + 2 * nt, base + nt : base + 2 * nt] = jnp.where(
+                same, jnp.broadcast_to(held[:, nt:], (nt, nt)), 0.0
+            )
+        out_ref[2 * nt :, : 2 * nt] = out_ref[: 2 * nt, 2 * nt :].T
 
 
 def pair_counts(rays, translations):
     angles, rows, width = rays.shape
     total = angles * translations
     return pl.pallas_call(
-        functools.partial(pair_kernel, translations=translations),
-        out_shape=jax.ShapeDtypeStruct((total, total), jnp.float32),
+        pair_kernel,
+        grid=(rows // 8,),
+        in_specs=[pl.BlockSpec((angles, 8, width), lambda i: (0, i, 0))],
+        out_specs=[
+            pl.BlockSpec((total, total), lambda i: (0, 0)),
+            pl.BlockSpec((8, total), lambda i: (0, 0)),
+        ],
+        out_shape=[
+            jax.ShapeDtypeStruct((total, total), jnp.float32),
+            jax.ShapeDtypeStruct((8, total), jnp.float32),
+        ],
         compiler_params=pltpu.CompilerParams(vmem_limit_bytes=40 * 1024 * 1024),
         cost_estimate=pl.CostEstimate(
-            flops=2 * total * total * rows * width, bytes_accessed=4 * total * total, transcendentals=0
+            flops=total * total * rows * width, bytes_accessed=4 * total * total, transcendentals=0
         ),
         name="pair_counts",
     )(rays)
+
+
+def greet(peers):
+    barrier = pltpu.get_barrier_semaphore()
+    for peer in peers:
+        pl.semaphore_signal(barrier, inc=1, device_id=peer, device_id_type=MESH)
+    pl.semaphore_wait(barrier, len(peers))
+
+
+def others(axis, size):
+    me = lax.axis_index(axis)
+    return [{axis: lax.rem(me + d, size)} for d in range(1, size)]
+
+
+def swap(axis, size, send, land, send_sem, recv_sem):
+    me = lax.axis_index(axis)
+    copies = [
+        pltpu.make_async_remote_copy(
+            src_ref=send,
+            dst_ref=land(me),
+            send_sem=send_sem.at[d],
+            recv_sem=recv_sem.at[d],
+            device_id={axis: lax.rem(me + d, size)},
+            device_id_type=MESH,
+        )
+        for d in range(1, size)
+    ]
+    for copy in copies:
+        copy.start()
+    return copies
+
+
+def gather_kernel(own_ref, all_ref, send_sem, recv_sem, *, scan, band, pix):
+    s, b, p = lax.axis_index("scan"), lax.axis_index("band"), lax.axis_index("pix")
+    greet(others("scan", scan) + others("band", band) + others("pix", pix))
+    all_ref[p, b, s] = own_ref[...]
+    for copy in swap(
+        "scan", scan, all_ref.at[p, b, s], lambda r: all_ref.at[p, b, r], send_sem.at[0], recv_sem.at[0]
+    ):
+        copy.wait()
+    for copy in swap(
+        "band", band, all_ref.at[p, b], lambda r: all_ref.at[p, r], send_sem.at[1], recv_sem.at[1]
+    ):
+        copy.wait()
+    for copy in swap("pix", pix, all_ref.at[p], lambda r: all_ref.at[r], send_sem.at[2], recv_sem.at[2]):
+        copy.wait()
+
+
+def gather_spectra(spectra, scan, band, pix):
+    comps, width = spectra.shape
+    most = max(scan, band, pix)
+    whole = pl.pallas_call(
+        functools.partial(gather_kernel, scan=scan, band=band, pix=pix),
+        out_shape=jax.ShapeDtypeStruct((pix, band, scan, comps, width), jnp.float32),
+        in_specs=[pl.BlockSpec(memory_space=pltpu.VMEM)],
+        out_specs=pl.BlockSpec(memory_space=pltpu.VMEM),
+        scratch_shapes=[pltpu.SemaphoreType.DMA((3, most)), pltpu.SemaphoreType.DMA((3, most))],
+        compiler_params=pltpu.CompilerParams(
+            collective_id=0, has_side_effects=True, vmem_limit_bytes=40 * 1024 * 1024
+        ),
+        name="gather_spectra",
+    )(spectra)
+    return whole.transpose(3, 2, 1, 0, 4).reshape(comps, scan * band * pix * width)
+
+
+def sirt_kernel(
+    part_ref, pairs_ref, count_ref, out_ref,
+    group, place, count_pix, count_mid, count_scan, proj, proj_pix, proj_mid, proj_scan,
+    send_sem, recv_sem, *, scan, band, pix, scale,
+):
+    s, b, p = lax.axis_index("scan"), lax.axis_index("band"), lax.axis_index("pix")
+    sizes = band * pix
+    rank = b * pix + p
+    group_peers = []
+    for d in range(1, sizes):
+        peer = lax.rem(rank + d, sizes)
+        group_peers.append({"band": lax.div(peer, pix), "pix": lax.rem(peer, pix)})
+    greet(group_peers + others("scan", scan))
+
+    copies = []
+    for d, peer in zip(range(1, sizes), group_peers):
+        copy = pltpu.make_async_remote_copy(
+            src_ref=part_ref.at[peer["band"]],
+            dst_ref=group.at[d],
+            send_sem=send_sem.at[0, d],
+            recv_sem=recv_sem.at[0, d],
+            device_id=peer,
+            device_id_type=MESH,
+        )
+        copy.start()
+        copies.append(copy)
+    copies += swap("pix", pix, count_ref, lambda r: count_pix.at[r], send_sem.at[1], recv_sem.at[1])
+    count_pix[p] = count_ref[...]
+    for copy in copies:
+        copy.wait()
+    value = part_ref[b]
+    for d in range(1, sizes):
+        value += group[d]
+    place[s] = value
+    counted = count_pix[0]
+    for r in range(1, pix):
+        counted += count_pix[r]
+    count_mid[...] = counted
+    count_scan[s] = counted
+    copies = swap("scan", scan, place.at[s], lambda r: place.at[r], send_sem.at[2], recv_sem.at[2])
+    copies += swap("scan", scan, count_mid, lambda r: count_scan.at[r], send_sem.at[3], recv_sem.at[3])
+    for copy in copies:
+        copy.wait()
+    counted = count_scan[0]
+    for r in range(1, scan):
+        counted += count_scan[r]
+    coefficients = jnp.concatenate([place[r] for r in range(scan)], axis=1)
+    comps, rays = coefficients.shape
+    ray_count = jnp.broadcast_to(counted[0:1], (comps, rays))
+    total = coefficients / ray_count
+    for k in range(ITERS - 1):
+        local = lax.dot_general(
+            total, pairs_ref[...], (((1,), (0,)), ((), ())),
+            precision=lax.Precision.HIGHEST, preferred_element_type=jnp.float32,
+        )
+        proj[k] = local
+        proj_pix[k, p] = local
+        for copy in swap(
+            "pix", pix, proj.at[k], lambda r: proj_pix.at[k, r], send_sem.at[4 + 2 * k], recv_sem.at[4 + 2 * k]
+        ):
+            copy.wait()
+        value = proj_pix[k, 0]
+        for r in range(1, pix):
+            value += proj_pix[k, r]
+        proj_mid[k] = value
+        proj_scan[k, s] = value
+        for copy in swap(
+            "scan", scan, proj_mid.at[k], lambda r: proj_scan.at[k, r], send_sem.at[5 + 2 * k], recv_sem.at[5 + 2 * k]
+        ):
+            copy.wait()
+        value = proj_scan[k, 0]
+        for r in range(1, scan):
+            value += proj_scan[k, r]
+        total += (coefficients - scale * value) / ray_count
+    out_ref[...] = total
+
+
+def sirt_table(parts, pairs, counts, scan, pix, scale):
+    band, comps, pos = parts.shape
+    rays = pairs.shape[0]
+    most = max(scan, band * pix)
+    steps = ITERS - 1
+    vmem = pl.BlockSpec(memory_space=pltpu.VMEM)
+    f32 = jnp.float32
+    return pl.pallas_call(
+        functools.partial(sirt_kernel, scan=scan, band=band, pix=pix, scale=scale),
+        out_shape=jax.ShapeDtypeStruct((comps, rays), f32),
+        in_specs=[vmem] * 3,
+        out_specs=vmem,
+        scratch_shapes=[
+            pltpu.VMEM((band * pix, comps, pos), f32),
+            pltpu.VMEM((scan, comps, pos), f32),
+            pltpu.VMEM((pix, 8, rays), f32),
+            pltpu.VMEM((8, rays), f32),
+            pltpu.VMEM((scan, 8, rays), f32),
+            pltpu.VMEM((steps, comps, rays), f32),
+            pltpu.VMEM((steps, pix, comps, rays), f32),
+            pltpu.VMEM((steps, comps, rays), f32),
+            pltpu.VMEM((steps, scan, comps, rays), f32),
+            pltpu.SemaphoreType.DMA((4 + 2 * steps, most)),
+            pltpu.SemaphoreType.DMA((4 + 2 * steps, most)),
+        ],
+        compiler_params=pltpu.CompilerParams(
+            collective_id=1, has_side_effects=True, vmem_limit_bytes=40 * 1024 * 1024
+        ),
+        name="sirt_table",
+    )(parts, pairs, counts)
 
 
 def back_kernel(table_ref, ray_ref, out_ref, *, translations):
@@ -162,36 +367,19 @@
     pos_total = pos_local * scan_count
     translations = pos_total // angles
     comp_local = comp_total // band_count
-    first_comp = lax.axis_index("band") * comp_local
-
-    copies = lax.axis_size("slices") * band_count
-    copy_id = lax.axis_index("slices") * band_count + lax.axis_index("band")
-    share = row_local // copies
-    own_rays = lax.dynamic_slice_in_dim(ray_index, copy_id * share, share, 1)
-    counts = lax.psum(pair_counts(own_rays, translations), ("slices", "scan", "band", "pix"))
-    all_spectra = lax.all_gather(spectra, ("scan", "band", "pix"), axis=1, tiled=True)
-
+
+    pix_count = lax.axis_size("pix")
+    all_spectra = gather_spectra(spectra, scan_count, band_count, pix_count)
+    pairs, counts = pair_counts(ray_index, translations)
     bins = bin_frames(frames, pixel_weight, pixel_slot, block_tile)
-
     gram = lax.dot_general(all_spectra, all_spectra, NT_DIMS, precision=highest)
     factor = jnp.linalg.cholesky(gram)
     moments_part = jnp.einsum(
         "ctl,tpl->cp", all_spectra.reshape(comp_total, Q // TILE, TILE), bins, precision=highest
     )
-    place = lax.axis_index("scan") * pos_local
-    moments_wide = lax.dynamic_update_slice_in_dim(
-        jnp.zeros((comp_total, pos_total), jnp.float32), moments_part, place, 1
-    )
-    moments = lax.psum(moments_wide, ("scan", "band", "pix"))
-    all_coefficients = jax.scipy.linalg.cho_solve((factor, True), moments)
-    coefficients = lax.dynamic_slice_in_dim(all_coefficients, first_comp, comp_local, 0)
-    ray_count = jnp.diagonal(counts)[None, :]
-    total = jnp.zeros((comp_local, pos_total), jnp.float32)
-    for sweep in range(ITERS):
-        residual = coefficients
-        if sweep > 0:
-            residual = coefficients - (RELAX / angles) * jnp.dot(total, counts, precision=highest)
-        total = total + residual / ray_count
+    parts = jax.scipy.linalg.cho_solve((factor, True), moments_part)
+    parts = parts.reshape(band_count, comp_local, pos_local)
+    total = sirt_table(parts, pairs, counts, scan_count, pix_count, RELAX / angles)
     return back_project((RELAX * img_width / angles) * total, ray_index, translations)
 
 

time: 320 us -> 119 us (0.37)
  waiting for transfers between devices: 202 us -> 0 us
  Pallas kernels: 47.5 us -> 100 us
  blocking collectives: 24.9 us -> 0 us
  between operations: 13.5 us -> 0.13 us
  local copies, waits for them, and re-layouts: 11.9 us -> 3.64 us
  matrix products: 7.14 us -> 1.96 us
    psum x2 -> x0, waiting for transfers between devices: 202 us -> none  [the longest x1 135 us: shards(): lax.psum(pair_counts(own_rays, translations), ('slices', 'scan', 'band',...]
    pallas_call x1 -> x3, Pallas kernels: 5.49 us -> 58.2 us  [the longest x1 27.9 us: sirt_table(): pl.pallas_call(functools.partial(sirt_kernel, scan=scan, band=band, pix=p...]
    all_gather x1 -> x0, blocking collectives: 24.9 us -> none  [shards(): lax.all_gather(spectra, ('scan', 'band', 'pix'), axis=1, tiled=True)]
    gather x1 -> x0, local copies, waits for them, and re-layouts: 8.42 us -> none  [shards(): ray_count = jnp.diagonal(counts)[None, :]]
    dot_general x2 -> x0, matrix products: 3.88 us -> none  [shards(): jnp.dot(total, counts, precision=highest)]
  transfers between devices with their start and end apart: 2 -> 0, of which waited for: 2 -> 0; matrix products, arithmetic and copies ran while one was open for 4% -> 0% of each run, Pallas kernels for 2% -> 0%
where the time goes in v2:
time: 119 us; the launch traced here: 118 us
  Pallas kernels  100 us (84%)
  other arithmetic  12.1 us (10%)
  local copies, waits for them, and re-layouts  3.64 us (3%)
  matrix products  1.96 us (2%)
    pallas_call x1, Pallas kernels, sirt_table(): pl.pallas_call(functools.partial(sirt_kernel, scan=scan, band=band, pix=p...  27.9 us
    pallas_call x1, Pallas kernels, bin_frames(): pl.pallas_call(functools.partial(bin_kernel, blocks=blocks), grid_spec=pl...  27.5 us
    pallas_call x1, Pallas kernels, pair_counts(): pl.pallas_call(pair_kernel, grid=(rows // 8,), in_specs=[pl.BlockSpec((an...  16 us
    pallas_call x1, Pallas kernels, back_project(): pl.pallas_call(functools.partial(back_kernel, translations=translations),...  14.7 us
    pallas_call x1, Pallas kernels, gather_spectra(): pl.pallas_call(functools.partial(gather_kernel, scan=scan, band=band, pix...  14.3 us
    another operation x3, other arithmetic, shards(): factor = jnp.linalg.cholesky(gram)  6.52 us
    another operation x2, other arithmetic, shards(): parts = jax.scipy.linalg.cho_solve((factor, True), moments_part)  5.55 us
    unnamed x10, local copies, waits for them, and re-layouts  3.49 us

profile of v2, /device:TPU:0, one launch (start us, length us, event | category | flops | bytes accessed | tf_op | source)
XLA Modules:
  0.0 118.2 jit_solution(9809331437697549181)
XLA Ops:
  0.0 0.0 copy-start.1
  0.0 0.0 copy-start.3
  0.0 0.8 copy-done.3
  0.8 14.3 %gather_spectra.1 = f32[2,2,4,64,128]{4,3,2,1,0:T(8,128)S(1)} custom-call(f32[64,128]{1,0:T(8,128)S(1)} %copy-done.3), custom_call_target="tpu_custom_call" | custom-call | tf_op jit(solution)/shard_map/gather_spectra/pallas_call | solution.py:194
  15.1 0.6 convolution_bitcast_fusion.2
  15.7 0.1 copy.12
  15.8 5.8 %cholesky.16 = f32[64,64]{1,0:T(8,128)S(1)} custom-call(f32[64,64]{1,0:T(8,128)S(1)} %fusion.2), custom_call_target="Cholesky" | custom-call | tf_op jit(solution)/shard_map/jit(cholesky)/cholesky | solution.py:376
  21.7 0.6 compare_reduce_fusion
  22.3 0.7 fusion
  23.0 4.9 %custom-call.10 = f32[1,64,64]{1,2,0:T(8,128)S(1)} custom-call(f32[1,64,64]{2,1,0:T(8,128)S(1)} %fusion), custom_call_target="InvertDiagBlocksLowerTriangular" | custom-call | tf_op jit(solution)/shard_map/jit(_cho_solve)/triangular_solve | solution.py:380
  27.9 0.0 copy-start
  27.9 1.0 copy-done
  29.0 0.0 copy-start.2
  29.0 0.9 copy-done.2
  29.9 0.0 copy-start.4
  29.9 0.7 copy-done.4
  30.6 27.5 %bin_frames.1 = f32[16,128,128]{2,1,0:T(8,128)S(1)} custom-call(s32[1024]{0:T(1024)S(1)} %copy-done.4, bf16[128,131072]{1,0:T(8,128)(2,1)} %frames_ref.1, s32[1024,128]{1,0:T(8,128)S(1)} %bitcast.34, bf16[1024,128]{1,0:T(8,128)(2,1)S(1)} %bitcast.35), custom_call_target="tpu_custom_call" | custom-call | flops 8589934592 | bytes 33554432 | tf_op jit(solution)/shard_map/bin_frames/pallas_call | solution.py:56
  58.1 1.0 convolution_bitcast_fusion
  59.1 0.3 convolution_bitcast_fusion.1
  59.4 0.2 fusion.4.part_ref
  59.5 0.0 copy-done.1
  59.5 16.0 %pair_counts.1 = (f32[512,512]{1,0:T(8,128)S(1)}, f32[8,512]{1,0:T(8,128)S(1)}) custom-call(s32[4,64,512]{2,1,0:T(8,128)S(1)} %copy-done.1), custom_call_target="tpu_custom_call" | custom-call | flops 8589934592 | bytes 1048576 | tf_op jit(solution)/shard_map/pair_counts/pallas_call | solution.py:125
  75.5 27.9 %sirt_table.1 = f32[32,512]{1,0:T(8,128)S(1)} custom-call(f32[2,32,128]{2,1,0:T(8,128)S(1)} %fusion.4.part_ref, f32[512,512]{1,0:T(8,128)S(1)} %get-tuple-element.7.pairs_ref, f32[8,512]{1,0:T(8,128)S(1)} %get-tuple-element.8.count_ref), custom_call_target="tpu_custom_call" | custom-call | tf_op jit(solution)/shard_map/sirt_table/pallas_call | solution.py:292
  103.5 14.7 %back_project.1 = f32[32,64,512]{2,1,0:T(8,128)} custom-call(f32[32,4,128]{2,1,0:T(4,128)S(1)} %reshape.27.table_ref, s32[4,64,512]{2,1,0:T(8,128)S(1)} %copy-done.1), custom_call_target="tpu_custom_call" | custom-call | flops 4194304 | bytes 4194304 | tf_op jit(solution)/shard_map/back_project/pallas_call | solution.py:343
  (5 shorter events, 0.1 us)
Async XLA Ops:
  0.0 59.5 %copy-start.1 = (s32[4,64,512]{2,1,0:T(8,128)S(1)}, s32[4,64,512]{2,1,0:T(8,128)}, u32[]{:S(2)}) copy-start(s32[4,64,512]{2,1,0:T(8,128)} %ray_ref.3) | copy-start | bytes 1572868
  0.0 0.8 copy-start.3
  27.9 1.0 copy-start
  29.0 0.9 copy-start.2
  29.9 0.7 copy-start.4

commit v3 on v2

--- a/solution.py
+++ b/solution.py
@@ -79,67 +79,50 @@
     )
 
 
-def pair_kernel(ray_ref, out_ref, count_ref):
-    step = pl.program_id(0)
+def meet(left, right):
+    return lax.dot_general(left, right, NT_DIMS, preferred_element_type=jnp.float32)
+
+
+def count_pairs(ray_ref, pair_ref, start, stop):
     angles, rows, width = ray_ref.shape
-    nt = out_ref.shape[0] // angles
-    row_id = lax.broadcasted_iota(jnp.int32, (nt, width), 0).astype(jnp.bfloat16)
-    one = jnp.ones((nt, width), jnp.bfloat16)
-    zero = jnp.zeros((nt, width), jnp.bfloat16)
-
-    @pl.when(step == 0)
-    def _():
-        out_ref[...] = jnp.zeros_like(out_ref)
-
-    def meet(left, right):
-        return lax.dot_general(left, right, NT_DIMS, preferred_element_type=jnp.float32)
-
-    for r in range(rows):
-        hits = []
-        for a in range(angles):
-            index = jnp.broadcast_to(ray_ref[a, r : r + 1, :].astype(jnp.float32), (nt, width))
-            hits.append(jnp.where(index.astype(jnp.bfloat16) == row_id, one, zero))
-        first = jnp.concatenate(hits[:2], axis=0)
-        last = jnp.concatenate(hits[2:], axis=0)
-        out_ref[: 2 * nt, 2 * nt :] += meet(first, last)
-        out_ref[:nt, : 2 * nt] += meet(hits[0], first)
-        out_ref[2 * nt : 3 * nt, 2 * nt :] += meet(hits[2], last)
-
-    @pl.when(step == pl.num_programs(0) - 1)
-    def _():
-        same = lax.broadcasted_iota(jnp.int32, (nt, nt), 0) == lax.broadcasted_iota(jnp.int32, (nt, nt), 1)
-        for base in (0, 2 * nt):
-            block = out_ref[base : base + nt, base : base + 2 * nt]
-            held = jnp.sum(block, axis=0, keepdims=True)
-            count_ref[:, base : base + 2 * nt] = jnp.broadcast_to(held, (8, 2 * nt))
-            out_ref[base + nt : base + 2 * nt, base : base + nt] = block[:, nt:].T
-            out_ref[base + nt : base + 2 * nt, base + nt : base + 2 * nt] = jnp.where(
-                same, jnp.broadcast_to(held[:, nt:], (nt, nt)), 0.0
-            )
-        out_ref[2 * nt :, : 2 * nt] = out_ref[: 2 * nt, 2 * nt :].T
-
-
-def pair_counts(rays, translations):
-    angles, rows, width = rays.shape
-    total = angles * translations
-    return pl.pallas_call(
-        pair_kernel,
-        grid=(rows // 8,),
-        in_specs=[pl.BlockSpec((angles, 8, width), lambda i: (0, i, 0))],
-        out_specs=[
-            pl.BlockSpec((total, total), lambda i: (0, 0)),
-            pl.BlockSpec((8, total), lambda i: (0, 0)),
-        ],
-        out_shape=[
-            jax.ShapeDtypeStruct((total, total), jnp.float32),
-            jax.ShapeDtypeStruct((8, total), jnp.float32),
-        ],
-        compiler_params=pltpu.CompilerParams(vmem_limit_bytes=40 * 1024 * 1024),
-        cost_estimate=pl.CostEstimate(
-            flops=total * total * rows * width, bytes_accessed=4 * total * total, transcendentals=0
-        ),
-        name="pair_counts",
-    )(rays)
+    nt = pair_ref.shape[0] // angles
+
+    def eight_rows(i, carry):
+        row_id = lax.broadcasted_iota(jnp.int32, (nt, width), 0).astype(jnp.bfloat16)
+        one = jnp.ones((nt, width), jnp.bfloat16)
+        zero = jnp.zeros((nt, width), jnp.bfloat16)
+        begin = pl.multiple_of(i * 8, 8)
+        held = [ray_ref[a, pl.ds(begin, 8), :].astype(jnp.float32) for a in range(angles)]
+        for r in range(8):
+            hits = []
+            for a in range(angles):
+                index = jnp.broadcast_to(held[a][r : r + 1, :], (nt, width))
+                hits.append(jnp.where(index.astype(jnp.bfloat16) == row_id, one, zero))
+            first = jnp.concatenate(hits[:2], axis=0)
+            last = jnp.concatenate(hits[2:], axis=0)
+            pair_ref[: 2 * nt, 2 * nt :] += meet(first, last)
+            pair_ref[:nt, : 2 * nt] += meet(hits[0], first)
+            pair_ref[2 * nt : 3 * nt, 2 * nt :] += meet(hits[2], last)
+        return carry
+
+    lax.fori_loop(start, stop, eight_rows, 0)
+
+
+def finish_pairs(pair_ref, high_ref, low_ref, count_ref, nt):
+    same = lax.broadcasted_iota(jnp.int32, (nt, nt), 0) == lax.broadcasted_iota(jnp.int32, (nt, nt), 1)
+    for base in (0, 2 * nt):
+        block = pair_ref[base : base + nt, base : base + 2 * nt]
+        held = jnp.sum(block, axis=0, keepdims=True)
+        count_ref[:, base : base + 2 * nt] = jnp.broadcast_to(held, (8, 2 * nt))
+        pair_ref[base + nt : base + 2 * nt, base : base + nt] = block[:, nt:].T
+        pair_ref[base + nt : base + 2 * nt, base + nt : base + 2 * nt] = jnp.where(
+            same, jnp.broadcast_to(held[:, nt:], (nt, nt)), 0.0
+        )
+    pair_ref[2 * nt :, : 2 * nt] = pair_ref[: 2 * nt, 2 * nt :].T
+    value = pair_ref[...]
+    high = jnp.floor(value * (1.0 / 256.0))
+    high_ref[...] = high.astype(jnp.bfloat16)
+    low_ref[...] = (value - 256.0 * high).astype(jnp.bfloat16)
 
 
 def greet(peers):
@@ -172,41 +155,65 @@
     return copies
 
 
-def gather_kernel(own_ref, all_ref, send_sem, recv_sem, *, scan, band, pix):
+def gather_kernel(
+    own_ref, ray_ref, all_ref, high_ref, low_ref, count_ref, pair_ref, send_sem, recv_sem, *, scan, band, pix
+):
     s, b, p = lax.axis_index("scan"), lax.axis_index("band"), lax.axis_index("pix")
+    groups = ray_ref.shape[1] // 8
+    cuts = [0, groups // 4, groups * 3 // 4, groups]
     greet(others("scan", scan) + others("band", band) + others("pix", pix))
     all_ref[p, b, s] = own_ref[...]
-    for copy in swap(
+    copies = swap(
         "scan", scan, all_ref.at[p, b, s], lambda r: all_ref.at[p, b, r], send_sem.at[0], recv_sem.at[0]
-    ):
+    )
+    pair_ref[...] = jnp.zeros_like(pair_ref)
+    count_pairs(ray_ref, pair_ref, cuts[0], cuts[1])
+    for copy in copies:
         copy.wait()
-    for copy in swap(
+    copies = swap(
         "band", band, all_ref.at[p, b], lambda r: all_ref.at[p, r], send_sem.at[1], recv_sem.at[1]
-    ):
+    )
+    count_pairs(ray_ref, pair_ref, cuts[1], cuts[2])
+    for copy in copies:
         copy.wait()
-    for copy in swap("pix", pix, all_ref.at[p], lambda r: all_ref.at[r], send_sem.at[2], recv_sem.at[2]):
+    copies = swap("pix", pix, all_ref.at[p], lambda r: all_ref.at[r], send_sem.at[2], recv_sem.at[2])
+    count_pairs(ray_ref, pair_ref, cuts[2], cuts[3])
+    finish_pairs(pair_ref, high_ref, low_ref, count_ref, pair_ref.shape[0] // ray_ref.shape[0])
+    for copy in copies:
         copy.wait()
 
 
-def gather_spectra(spectra, scan, band, pix):
+def gather_spectra(spectra, rays, translations, scan, band, pix):
     comps, width = spectra.shape
     most = max(scan, band, pix)
-    whole = pl.pallas_call(
+    total = rays.shape[0] * translations
+    vmem = pl.BlockSpec(memory_space=pltpu.VMEM)
+    whole, high, low, counts = pl.pallas_call(
         functools.partial(gather_kernel, scan=scan, band=band, pix=pix),
-        out_shape=jax.ShapeDtypeStruct((pix, band, scan, comps, width), jnp.float32),
-        in_specs=[pl.BlockSpec(memory_space=pltpu.VMEM)],
-        out_specs=pl.BlockSpec(memory_space=pltpu.VMEM),
-        scratch_shapes=[pltpu.SemaphoreType.DMA((3, most)), pltpu.SemaphoreType.DMA((3, most))],
+        out_shape=[
+            jax.ShapeDtypeStruct((pix, band, scan, comps, width), jnp.float32),
+            jax.ShapeDtypeStruct((total, total), jnp.bfloat16),
+            jax.ShapeDtypeStruct((total, total), jnp.bfloat16),
+            jax.ShapeDtypeStruct((8, total), jnp.float32),
+        ],
+        in_specs=[vmem] * 2,
+        out_specs=[vmem] * 4,
+        scratch_shapes=[
+            pltpu.VMEM((total, total), jnp.float32),
+            pltpu.SemaphoreType.DMA((3, most)),
+            pltpu.SemaphoreType.DMA((3, most)),
+        ],
         compiler_params=pltpu.CompilerParams(
             collective_id=0, has_side_effects=True, vmem_limit_bytes=40 * 1024 * 1024
         ),
         name="gather_spectra",
-    )(spectra)
-    return whole.transpose(3, 2, 1, 0, 4).reshape(comps, scan * band * pix * width)
+    )(spectra, rays)
+    spread = whole.transpose(3, 2, 1, 0, 4).reshape(comps, scan * band * pix * width)
+    return spread, high, low, counts
 
 
 def sirt_kernel(
-    part_ref, pairs_ref, count_ref, out_ref,
+    part_ref, high_ref, low_ref, count_ref, out_ref,
     group, place, count_pix, count_mid, count_scan, proj, proj_pix, proj_mid, proj_scan,
     send_sem, recv_sem, *, scan, band, pix, scale,
 ):
@@ -256,10 +263,13 @@
     ray_count = jnp.broadcast_to(counted[0:1], (comps, rays))
     total = coefficients / ray_count
     for k in range(ITERS - 1):
-        local = lax.dot_general(
-            total, pairs_ref[...], (((1,), (0,)), ((), ())),
-            precision=lax.Precision.HIGHEST, preferred_element_type=jnp.float32,
-        )
+        lead = total.astype(jnp.bfloat16).astype(jnp.float32)
+        rest = total - lead
+        middle = rest.astype(jnp.bfloat16).astype(jnp.float32)
+        pieces = jnp.concatenate([lead, middle, rest - middle], axis=0).astype(jnp.bfloat16)
+        both = 256.0 * jnp.dot(pieces, high_ref[...], preferred_element_type=jnp.float32)
+        both += jnp.dot(pieces, low_ref[...], preferred_element_type=jnp.float32)
+        local = both[:comps] + (both[comps : 2 * comps] + both[2 * comps :])
         proj[k] = local
         proj_pix[k, p] = local
         for copy in swap(
@@ -282,9 +292,9 @@
     out_ref[...] = total
 
 
-def sirt_table(parts, pairs, counts, scan, pix, scale):
+def sirt_table(parts, high, low, counts, scan, pix, scale):
     band, comps, pos = parts.shape
-    rays = pairs.shape[0]
+    rays = high.shape[0]
     most = max(scan, band * pix)
     steps = ITERS - 1
     vmem = pl.BlockSpec(memory_space=pltpu.VMEM)
@@ -292,7 +302,7 @@
     return pl.pallas_call(
         functools.partial(sirt_kernel, scan=scan, band=band, pix=pix, scale=scale),
         out_shape=jax.ShapeDtypeStruct((comps, rays), f32),
-        in_specs=[vmem] * 3,
+        in_specs=[vmem] * 4,
         out_specs=vmem,
         scratch_shapes=[
             pltpu.VMEM((band * pix, comps, pos), f32),
@@ -311,29 +321,28 @@
             collective_id=1, has_side_effects=True, vmem_limit_bytes=40 * 1024 * 1024
         ),
         name="sirt_table",
-    )(parts, pairs, counts)
+    )(parts, high, low, counts)
 
 
 def back_kernel(table_ref, ray_ref, out_ref, *, translations):
     comps, rows, width = out_ref.shape
     angles = ray_ref.shape[0]
 
-    def one_comp(c, carry):
-        rows_of = table_ref[c]
-        tables = [jnp.broadcast_to(rows_of[a : a + 1, :], (8, translations)) for a in range(angles)]
-        for r in range(0, rows, 8):
-            for w in range(0, width, translations):
-                value = None
-                for a in range(angles):
-                    index = ray_ref[a, r : r + 8, w : w + translations]
-                    got = jnp.take_along_axis(
-                        tables[a], index, axis=1, mode="promise_in_bounds"
-                    )
-                    value = got if value is None else value + got
-                out_ref[c, r : r + 8, w : w + translations] = value
+    def eight_rows(i, carry):
+        begin = pl.multiple_of(i * 8, 8)
+        for w in range(0, width, translations):
+            values = [None] * comps
+            for a in range(angles):
+                index = ray_ref[a, pl.ds(begin, 8), w : w + translations]
+                for c in range(comps):
+                    table = jnp.broadcast_to(table_ref[c, a : a + 1, :], (8, translations))
+                    got = jnp.take_along_axis(table, index, axis=1, mode="promise_in_bounds")
+                    values[c] = got if a == 0 else values[c] + got
+            for c in range(comps):
+                out_ref[c, pl.ds(begin, 8), w : w + translations] = values[c]
         return carry
 
-    lax.fori_loop(0, comps, one_comp, 0)
+    lax.fori_loop(0, rows // 8, eight_rows, 0)
 
 
 def back_project(table, rays, translations):
@@ -369,8 +378,9 @@
     comp_local = comp_total // band_count
 
     pix_count = lax.axis_size("pix")
-    all_spectra = gather_spectra(spectra, scan_count, band_count, pix_count)
-    pairs, counts = pair_counts(ray_index, translations)
+    all_spectra, high, low, counts = gather_spectra(
+        spectra, ray_index, translations, scan_count, band_count, pix_count
+    )
     bins = bin_frames(frames, pixel_weight, pixel_slot, block_tile)
     gram = lax.dot_general(all_spectra, all_spectra, NT_DIMS, precision=highest)
     factor = jnp.linalg.cholesky(gram)
@@ -379,7 +389,7 @@
     )
     parts = jax.scipy.linalg.cho_solve((factor, True), moments_part)
     parts = parts.reshape(band_count, comp_local, pos_local)
-    total = sirt_table(parts, pairs, counts, scan_count, pix_count, RELAX / angles)
+    total = sirt_table(parts, high, low, counts, scan_count, pix_count, RELAX / angles)
     return back_project((RELAX * img_width / angles) * total, ray_index, translations)
 
 

time: 119 us -> 103 us (0.87)
  Pallas kernels: 100 us -> 85.5 us
    pallas_call x1 -> x0, Pallas kernels: 16 us -> none  [pair_counts(): pl.pallas_call(pair_kernel, grid=(rows // 8,), in_specs=[pl.BlockSpec((an...]
    pallas_call x1, Pallas kernels: 14.3 us -> 21.2 us  [gather_spectra(): pl.pallas_call(functools.partial(gather_kernel, scan=scan, band=band, pix...]
    pallas_call x1, Pallas kernels: 14.7 us -> 9.16 us  [back_project(): pl.pallas_call(functools.partial(back_kernel, translations=translations),...]
where the time goes in v3:
time: 103 us
  Pallas kernels  85.5 us (83%)
  other arithmetic  12.1 us (12%)
  local copies, waits for them, and re-layouts  2.89 us (3%)
  matrix products  2.16 us (2%)
    pallas_call x1, Pallas kernels, sirt_table(): pl.pallas_call(functools.partial(sirt_kernel, scan=scan, band=band, pix=p...  27.7 us
    pallas_call x1, Pallas kernels, bin_frames(): pl.pallas_call(functools.partial(bin_kernel, blocks=blocks), grid_spec=pl...  27.4 us
    pallas_call x1, Pallas kernels, gather_spectra(): pl.pallas_call(functools.partial(gather_kernel, scan=scan, band=band, pix...  21.2 us
    pallas_call x1, Pallas kernels, back_project(): pl.pallas_call(functools.partial(back_kernel, translations=translations),...  9.16 us
    another operation x3, other arithmetic, shards(): factor = jnp.linalg.cholesky(gram)  6.52 us
    another operation x2, other arithmetic, shards(): parts = jax.scipy.linalg.cho_solve((factor, True), moments_part)  5.55 us
    unnamed x10, local copies, waits for them, and re-layouts  2.74 us

profile of v3, /device:TPU:0, one launch (start us, length us, event | category | flops | bytes accessed | tf_op | source)
XLA Modules:
  0.0 102.7 jit_solution(509772757129226000)
XLA Ops:
  0.0 0.0 copy-start
  0.0 0.0 copy-start.1
  0.0 1.1 %copy-done.1 = s32[131072]{0:T(1024)S(1)} copy-done((s32[131072]{0:T(1024)S(1)}, s32[131072]{0:T(1024)}, u32[]{:S(2)}) %copy-start.1) | copy-done | bytes 524312
  1.1 0.0 copy-start.2
  1.1 0.9 copy-done.2
  2.1 0.0 copy-start.4
  2.1 0.7 copy-done.4
  2.7 0.0 copy-start.3
  2.7 27.4 %bin_frames.1 = f32[16,128,128]{2,1,0:T(8,128)S(1)} custom-call(s32[1024]{0:T(1024)S(1)} %copy-done.4, bf16[128,131072]{1,0:T(8,128)(2,1)} %frames_ref.1, s32[1024,128]{1,0:T(8,128)S(1)} %bitcast.34, bf16[1024,128]{1,0:T(8,128)(2,1)S(1)} %bitcast.35), custom_call_target="tpu_custom_call" | custom-call | flops 8589934592 | bytes 33554432 | tf_op jit(solution)/shard_map/bin_frames/pallas_call | solution.py:56
  30.2 0.0 copy-done
  30.2 0.0 copy-done.3
  30.2 21.2 %gather_spectra.1 = (f32[2,2,4,64,128]{4,3,2,1,0:T(8,128)S(1)}, bf16[512,512]{1,0:T(8,128)(2,1)S(1)}, bf16[512,512]{1,0:T(8,128)(2,1)S(1)}, f32[8,512]{1,0:T(8,128)S(1)}) custom-call(f32[64,128]{1,0:T(8,128)S(1)} %copy-done.3, s32[4,64,512]{2,1,0:T(8,128)S(1)} %copy-done), custom_call_target="tpu_custom_call" | custom-call | tf_op jit(solution)/shard_map/gather_spectra/pallas_call | solution.py:191
  51.4 0.6 convolution_bitcast_fusion.2
  52.0 0.1 copy.12
  52.1 5.8 %cholesky.16 = f32[64,64]{1,0:T(8,128)S(1)} custom-call(f32[64,64]{1,0:T(8,128)S(1)} %fusion.2), custom_call_target="Cholesky" | custom-call | tf_op jit(solution)/shard_map/jit(cholesky)/cholesky | solution.py:386
  58.0 0.6 compare_reduce_fusion
  58.6 0.7 fusion
  59.3 4.9 %custom-call.10 = f32[1,64,64]{1,2,0:T(8,128)S(1)} custom-call(f32[1,64,64]{2,1,0:T(8,128)S(1)} %fusion), custom_call_target="InvertDiagBlocksLowerTriangular" | custom-call | tf_op jit(solution)/shard_map/jit(_cho_solve)/triangular_solve | solution.py:390
  64.2 1.2 %convolution_bitcast_fusion = f32[64,128]{1,0:T(8,128)S(1)} fusion(f32[64,16,128]{2,0,1:T(8,128)S(1)} %bitcast.36, f32[16,128,128]{2,1,0:T(8,128)S(1)} %bin_frames.1), kind=kOutput, calls=%fused_computation | convolution fusion | flops 201326592 | bytes 1605632 | tf_op jit(solution)/shard_map/ctl,tpl->cp/dot_general | solution.py:387
  65.5 0.2 convolution_bitcast_fusion.1
  65.7 0.2 fusion.4.part_ref
  65.9 27.7 %sirt_table.1 = f32[32,512]{1,0:T(8,128)S(1)} custom-call(f32[2,32,128]{2,1,0:T(8,128)S(1)} %fusion.4.part_ref, bf16[512,512]{1,0:T(8,128)(2,1)S(1)} %get-tuple-element.10.high_ref, bf16[512,512]{1,0:T(8,128)(2,1)S(1)} %get-tuple-element.11.low_ref, f32[8,512]{1,0:T(8,128)S(1)} %get-tuple-element.12.count_ref), custom_call_target="tpu_custom_call" | custom-call | tf_op jit(solution)/shard_map/sirt_table/pallas_call | solution.py:302
  93.6 9.2 %back_project.1 = f32[32,64,512]{2,1,0:T(8,128)} custom-call(f32[32,4,128]{2,1,0:T(4,128)S(1)} %reshape.27.table_ref, s32[4,64,512]{2,1,0:T(8,128)S(1)} %copy-done), custom_call_target="tpu_custom_call" | custom-call | flops 4194304 | bytes 4194304 | tf_op jit(solution)/shard_map/back_project/pallas_call | solution.py:352
  (5 shorter events, 0.1 us)
Async XLA Ops:
  0.0 30.2 %copy-start = (s32[4,64,512]{2,1,0:T(8,128)S(1)}, s32[4,64,512]{2,1,0:T(8,128)}, u32[]{:S(2)}) copy-start(s32[4,64,512]{2,1,0:T(8,128)} %ray_ref.3) | copy-start | bytes 1572868
  0.0 1.1 %copy-start.1 = (s32[131072]{0:T(1024)S(1)}, s32[131072]{0:T(1024)}, u32[]{:S(2)}) copy-start(s32[131072]{0:T(1024)} %param.8) | copy-start | bytes 1572868
  1.1 0.9 copy-start.2
  2.1 0.7 copy-start.4
  2.7 27.5 %copy-start.3 = (f32[64,128]{1,0:T(8,128)S(1)}, f32[64,128]{1,0:T(8,128)}, u32[]{:S(2)}) copy-start(f32[64,128]{1,0:T(8,128)} %own_ref.1) | copy-start | bytes 98308

commit v4 on v3

--- a/solution.py
+++ b/solution.py
@@ -11,7 +11,7 @@
 Q = 2048
 ITERS = 3
 RELAX = 1.5
-CHUNK = 8192
+CHUNK = 16384
 MESH = pl.DeviceIdType.MESH
 NT_DIMS = (((1,), (1,)), ((), ()))
 

time: 103 us -> 102 us (level)
  Pallas kernels: 85.5 us -> 84.4 us
    pallas_call x1, Pallas kernels: 27.4 us -> 26.4 us  [bin_frames(): pl.pallas_call(functools.partial(bin_kernel, blocks=blocks), grid_spec=pl...]
where the time goes in v4:
time: 102 us
  Pallas kernels  84.4 us (83%)
  other arithmetic  12.1 us (12%)
  local copies, waits for them, and re-layouts  2.89 us (3%)
  matrix products  2.16 us (2%)
    pallas_call x1, Pallas kernels, sirt_table(): pl.pallas_call(functools.partial(sirt_kernel, scan=scan, band=band, pix=p...  27.6 us
    pallas_call x1, Pallas kernels, bin_frames(): pl.pallas_call(functools.partial(bin_kernel, blocks=blocks), grid_spec=pl...  26.4 us
    pallas_call x1, Pallas kernels, gather_spectra(): pl.pallas_call(functools.partial(gather_kernel, scan=scan, band=band, pix...  21.3 us
    pallas_call x1, Pallas kernels, back_project(): pl.pallas_call(functools.partial(back_kernel, translations=translations),...  9.16 us
    another operation x3, other arithmetic, shards(): factor = jnp.linalg.cholesky(gram)  6.52 us
    another operation x2, other arithmetic, shards(): parts = jax.scipy.linalg.cho_solve((factor, True), moments_part)  5.55 us
    unnamed x10, local copies, waits for them, and re-layouts  2.74 us

profile of v4, /device:TPU:0, one launch (start us, length us, event | category | flops | bytes accessed | tf_op | source)
XLA Modules:
  0.0 101.7 jit_solution(16615459187348293593)
XLA Ops:
  0.0 0.0 copy-start
  0.0 0.0 copy-start.1
  0.0 1.1 %copy-done.1 = s32[131072]{0:T(1024)S(1)} copy-done((s32[131072]{0:T(1024)S(1)}, s32[131072]{0:T(1024)}, u32[]{:S(2)}) %copy-start.1) | copy-done | bytes 524312
  1.1 0.0 copy-start.2
  1.1 0.9 copy-done.2
  2.1 0.0 copy-start.4
  2.1 0.7 copy-done.4
  2.7 0.0 copy-start.3
  2.7 26.4 %bin_frames.1 = f32[16,128,128]{2,1,0:T(8,128)S(1)} custom-call(s32[1024]{0:T(1024)S(1)} %copy-done.4, bf16[128,131072]{1,0:T(8,128)(2,1)} %frames_ref.1, s32[1024,128]{1,0:T(8,128)S(1)} %bitcast.34, bf16[1024,128]{1,0:T(8,128)(2,1)S(1)} %bitcast.35), custom_call_target="tpu_custom_call" | custom-call | flops 8589934592 | bytes 33554432 | tf_op jit(solution)/shard_map/bin_frames/pallas_call | solution.py:56
  29.1 0.0 copy-done
  29.2 0.0 copy-done.3
  29.2 21.3 %gather_spectra.1 = (f32[2,2,4,64,128]{4,3,2,1,0:T(8,128)S(1)}, bf16[512,512]{1,0:T(8,128)(2,1)S(1)}, bf16[512,512]{1,0:T(8,128)(2,1)S(1)}, f32[8,512]{1,0:T(8,128)S(1)}) custom-call(f32[64,128]{1,0:T(8,128)S(1)} %copy-done.3, s32[4,64,512]{2,1,0:T(8,128)S(1)} %copy-done), custom_call_target="tpu_custom_call" | custom-call | tf_op jit(solution)/shard_map/gather_spectra/pallas_call | solution.py:191
  50.4 0.6 convolution_bitcast_fusion.2
  51.0 0.1 copy.12
  51.1 5.8 %cholesky.16 = f32[64,64]{1,0:T(8,128)S(1)} custom-call(f32[64,64]{1,0:T(8,128)S(1)} %fusion.2), custom_call_target="Cholesky" | custom-call | tf_op jit(solution)/shard_map/jit(cholesky)/cholesky | solution.py:386
  57.0 0.6 compare_reduce_fusion
  57.6 0.7 fusion
  58.3 4.9 %custom-call.10 = f32[1,64,64]{1,2,0:T(8,128)S(1)} custom-call(f32[1,64,64]{2,1,0:T(8,128)S(1)} %fusion), custom_call_target="InvertDiagBlocksLowerTriangular" | custom-call | tf_op jit(solution)/shard_map/jit(_cho_solve)/triangular_solve | solution.py:390
  63.2 1.2 %convolution_bitcast_fusion = f32[64,128]{1,0:T(8,128)S(1)} fusion(f32[64,16,128]{2,0,1:T(8,128)S(1)} %bitcast.36, f32[16,128,128]{2,1,0:T(8,128)S(1)} %bin_frames.1), kind=kOutput, calls=%fused_computation | convolution fusion | flops 201326592 | bytes 1605632 | tf_op jit(solution)/shard_map/ctl,tpl->cp/dot_general | solution.py:387
  64.4 0.2 convolution_bitcast_fusion.1
  64.7 0.2 fusion.4.part_ref
  64.8 27.6 %sirt_table.1 = f32[32,512]{1,0:T(8,128)S(1)} custom-call(f32[2,32,128]{2,1,0:T(8,128)S(1)} %fusion.4.part_ref, bf16[512,512]{1,0:T(8,128)(2,1)S(1)} %get-tuple-element.10.high_ref, bf16[512,512]{1,0:T(8,128)(2,1)S(1)} %get-tuple-element.11.low_ref, f32[8,512]{1,0:T(8,128)S(1)} %get-tuple-element.12.count_ref), custom_call_target="tpu_custom_call" | custom-call | tf_op jit(solution)/shard_map/sirt_table/pallas_call | solution.py:302
  92.5 9.2 %back_project.1 = f32[32,64,512]{2,1,0:T(8,128)} custom-call(f32[32,4,128]{2,1,0:T(4,128)S(1)} %reshape.27.table_ref, s32[4,64,512]{2,1,0:T(8,128)S(1)} %copy-done), custom_call_target="tpu_custom_call" | custom-call | flops 4194304 | bytes 4194304 | tf_op jit(solution)/shard_map/back_project/pallas_call | solution.py:352
  (5 shorter events, 0.1 us)
Async XLA Ops:
  0.0 29.1 %copy-start = (s32[4,64,512]{2,1,0:T(8,128)S(1)}, s32[4,64,512]{2,1,0:T(8,128)}, u32[]{:S(2)}) copy-start(s32[4,64,512]{2,1,0:T(8,128)} %ray_ref.3) | copy-start | bytes 1572868
  0.0 1.1 %copy-start.1 = (s32[131072]{0:T(1024)S(1)}, s32[131072]{0:T(1024)}, u32[]{:S(2)}) copy-start(s32[131072]{0:T(1024)} %param.8) | copy-start | bytes 1572868
  1.1 0.9 copy-start.2
  2.1 0.7 copy-start.4
  2.7 26.4 %copy-start.3 = (f32[64,128]{1,0:T(8,128)S(1)}, f32[64,128]{1,0:T(8,128)}, u32[]{:S(2)}) copy-start(f32[64,128]{1,0:T(8,128)} %own_ref.1) | copy-start | bytes 98308
